TPU v7x, 256 devices: a whole 4x4x8 slice. The times are simulated.
256 devices in a mesh: row: 16 (over y, x), col: 8 (over z), depth: 2 (over core).
Axes of the slice: x: 4, y: 4, z: 8, core: 2. Of those that a mesh axis runs over, the one named last changes fastest.
Arguments:
- ham_blocks: bfloat16 [512, 8, 128, 128], P(('row', 'depth'), 'col'), may hold values from -0.25 to 0.25
- deriv_blocks: bfloat16 [512, 8, 128, 128], P(('row', 'depth'), 'col'), may hold values from -0.25 to 0.25
- ham_cols: int32 [512, 8], P(('row', 'depth')), may hold values from 0 to 511, as said below
- cheb_prev: bfloat16 [32, 64, 128, 128], P('col', 'row'), may hold values from -6 to 6
- cheb_cur: bfloat16 [32, 64, 128, 128], P('col', 'row'), may hold values from -6 to 6
- tang_prev: bfloat16 [32, 64, 128, 128], P('col', 'row'), may hold values from -6 to 6
- tang_cur: bfloat16 [32, 64, 128, 128], P('col', 'row'), may hold values from -6 to 6
- cheb_rows: int32 [32, 64], P('col'), may hold values from 0 to 511, as said below
- keep_mask: int32 [32, 64], P('col', 'row'), may hold values 0 or 1
Outputs:
- cheb_last: bfloat16 [32, 64, 128, 128], P('col', 'row')
- tang_last: bfloat16 [32, 64, 128, 128], P('col', 'row')
Inputs may be any that keep to these rules, and one draw needn't show every extreme that they name: `ham_cols`: each block row lists 8 different block columns, 1 of them in each of the 8 ranges of 64 columns, the ranges in order along the slots. `cheb_rows`: each window column lists 64 different block rows, 2 of them in each of the 32 ranges of 16 rows, the ranges in order along the slots.
All inputs are finite; a program needn't handle non-finite values. No bound on the sum of `keep_mask` on one device may be relied on, other than what follows from the above.
Results may differ from a plain program's by a relative error of at most 0.0042.
Values may be sent and summed in bfloat16 or wider, within the bound.
No kernel may reach another device: no remote copies, remote signals or barrier semaphores. Data moves between devices by JAX's collectives and lax.ppermute only.
A program may use at most 128 MiB of HBM per device.

v0:
```python
import jax
import jax.numpy as jnp
from jax import lax
from jax.sharding import PartitionSpec as P


def pick_blocks(blocks, index):
    return jnp.take(blocks, index, axis=0)


def select_terms(ham_piece, deriv_piece, cols_piece, row_index, cheb_panel, tang_panel, cheb_rows):
    picked_ham = jnp.take(ham_piece, row_index, axis=0)
    picked_deriv = jnp.take(deriv_piece, row_index, axis=0)
    needed = jnp.take(cols_piece, row_index, axis=0)
    equal = needed[:, :, :, None] == cheb_rows[:, None, None, :]
    found = jnp.any(equal, axis=-1)[:, :, :, None, None]
    position = jnp.argmax(equal, axis=-1)
    gather_cols = jax.vmap(pick_blocks)
    zero_block = jnp.zeros((), jnp.bfloat16)
    picked_cheb = jnp.where(found, gather_cols(cheb_panel, position), zero_block)
    picked_tang = jnp.where(found, gather_cols(tang_panel, position), zero_block)
    prod_cheb = jnp.einsum(
        "jsqab,jsqbc->jsac", picked_ham, picked_cheb, preferred_element_type=jnp.float32
    )
    prod_tang = jnp.einsum(
        "jsqab,jsqbc->jsac", picked_deriv, picked_cheb, preferred_element_type=jnp.float32
    )
    prod_tang = prod_tang + jnp.einsum(
        "jsqab,jsqbc->jsac", picked_ham, picked_tang, preferred_element_type=jnp.float32
    )
    return (prod_cheb, prod_tang)


def on_device(
    ham_blocks,
    deriv_blocks,
    ham_cols,
    cheb_prev,
    cheb_cur,
    tang_prev,
    tang_cur,
    cheb_rows,
    keep_mask,
):
    layers = lax.axis_size("depth")
    layer_index = lax.axis_index("depth")
    row_group = lax.axis_index("row")
    slots_row = cheb_cur.shape[1]
    slots_group = slots_row // layers
    ham_rows, deriv_rows, cols_rows = (ham_blocks, deriv_blocks, ham_cols)
    rows_here = ham_rows.shape[0]
    group = row_group * layers + layer_index
    slot_start = group * slots_group
    old_offset = layer_index * slots_group
    row_base = slot_start // slots_group * rows_here
    mine = lax.dynamic_slice_in_dim(cheb_rows, slot_start, slots_group, 1)
    row_index = mine - row_base
    keep = lax.dynamic_slice_in_dim(keep_mask, old_offset, slots_group, 1).astype(jnp.float32)[
        :, :, None, None
    ]
    ham_panel, deriv_panel = (
        lax.all_gather(ham_rows, "col", axis=1, tiled=True),
        lax.all_gather(deriv_rows, "col", axis=1, tiled=True),
    )

    def products(cheb_panel, tang_panel):
        return select_terms(
            ham_panel, deriv_panel, cols_rows, row_index, cheb_panel, tang_panel, cheb_rows
        )

    def own_part(blocks):
        return lax.dynamic_slice_in_dim(blocks, old_offset, slots_group, 1).astype(jnp.float32)

    def update(prod_cheb, prod_tang, cheb_old, tang_old):
        cheb_new = (keep * (2.0 * prod_cheb - own_part(cheb_old))).astype(jnp.bfloat16)
        tang_new = (keep * (2.0 * prod_tang - own_part(tang_old))).astype(jnp.bfloat16)
        return (cheb_new, tang_new)

    cheb_panel, tang_panel = (
        lax.all_gather(cheb_cur, "row", axis=1, tiled=True),
        lax.all_gather(tang_cur, "row", axis=1, tiled=True),
    )
    prod_cheb, prod_tang = products(cheb_panel, tang_panel)
    cheb_mid, tang_mid = update(prod_cheb, prod_tang, cheb_prev, tang_prev)
    cheb_full, tang_full = (
        lax.all_gather(cheb_mid, "depth", axis=1, tiled=True),
        lax.all_gather(tang_mid, "depth", axis=1, tiled=True),
    )
    cheb_panel, tang_panel = (
        lax.all_gather(cheb_full, "row", axis=1, tiled=True),
        lax.all_gather(tang_full, "row", axis=1, tiled=True),
    )
    prod_cheb, prod_tang = products(cheb_panel, tang_panel)
    cheb_new, tang_new = update(prod_cheb, prod_tang, cheb_cur, tang_cur)
    cheb_last, tang_last = (
        lax.all_gather(cheb_new, "depth", axis=1, tiled=True),
        lax.all_gather(tang_new, "depth", axis=1, tiled=True),
    )
    return (cheb_last, tang_last)


def solution(mesh):
    placed = (
        P(("row", "depth"), "col", None, None),
        P(("row", "depth"), "col", None, None),
        P(("row", "depth"), None),
        P("col", "row", None, None),
        P("col", "row", None, None),
        P("col", "row", None, None),
        P("col", "row", None, None),
        P("col", None),
        P("col", "row"),
    )
    return jax.shard_map(
        on_device,
        mesh=mesh,
        in_specs=placed,
        out_specs=(P("col", "row", None, None), P("col", "row", None, None)),
        check_vma=False,
    )
```

profile of v0, /device:TPU:1, one launch (start us, length us, event | category | flops | bytes accessed | tf_op | source)
XLA Modules:
  0.0 451.9 jit_solution(9809406284382215170)
XLA Ops:
  7.2 0.0 all-gather.7.cloned.1.call-start
  7.2 0.7 all-gather.7.cloned.1.call-update
  7.9 0.0 all-gather.9.cloned.1.call-start
  8.0 0.7 all-gather.9.cloned.1.call-update
  8.7 0.0 all-gather.13.cloned.1.call-start
  8.7 0.7 all-gather.13.cloned.1.call-update
  9.4 0.0 all-gather.15.cloned.1.call-start
  9.5 0.5 all-gather.15.cloned.1.call-update
  10.0 0.0 all-gather.11.cloned.1.call-start
  10.1 0.1 copy.12
  10.1 0.1 compare_and_fusion.1
  10.2 0.1 reshape.97
  10.3 0.6 gather_fusion.1
  10.9 0.1 broadcast_select_fusion.56
  10.9 1.0 compare_reduce_fusion
  12.0 0.1 reshape.106
  12.1 0.1 dynamic-slice_convert_fusion
  12.2 0.3 compare_reduce_fusion.1
  12.5 56.0 %all-gather.7.cloned.1.call-done = bf16[16,8,128,128]{3,2,1,0:T(8,128)(2,1)} async-done(((bf16[16,1,128,128]{3,2,1,0:T(8,128)(2,1)}), bf16[16,8,128,128]{3,2,1,0:T(8,128)(2,1)}) %all-gather.7.cloned.1.call-update) | async-done | bytes 4194320 | tf_op jit(solution)/shard_map/all_gather | solution.py:62
  68.5 4.4 gather_fusion
  72.9 72.5 %all-gather.9.cloned.1.call-done = bf16[4,64,128,128]{3,2,1,0:T(8,128)(2,1)} async-done(((bf16[4,4,128,128]{3,2,1,0:T(8,128)(2,1)}), bf16[4,64,128,128]{3,2,1,0:T(8,128)(2,1)}) %all-gather.9.cloned.1.call-update) | async-done | bytes 8388624 | tf_op jit(solution)/shard_map/all_gather | solution.py:80
  145.3 4.3 gather_fusion.2
  149.7 2.4 fusion.30
  152.1 2.6 all_gather.32
  154.7 0.0 all-gather.11.cloned.1.call-update
  154.8 0.0 all-gather.17.cloned.1.call-start
  154.8 46.9 %all-gather.13.cloned.1.call-done = bf16[16,8,128,128]{3,2,1,0:T(8,128)(2,1)} async-done(((bf16[16,1,128,128]{3,2,1,0:T(8,128)(2,1)}), bf16[16,8,128,128]{3,2,1,0:T(8,128)(2,1)}) %all-gather.13.cloned.1.call-update) | async-done | bytes 4194320 | tf_op jit(solution)/shard_map/all_gather | solution.py:63
  201.7 4.3 gather_fusion.4
  206.0 72.3 %all-gather.15.cloned.1.call-done = bf16[4,64,128,128]{3,2,1,0:T(8,128)(2,1)} async-done(((bf16[4,4,128,128]{3,2,1,0:T(8,128)(2,1)}), bf16[4,64,128,128]{3,2,1,0:T(8,128)(2,1)}) %all-gather.15.cloned.1.call-update) | async-done | bytes 8388624 | tf_op jit(solution)/shard_map/all_gather | solution.py:81
  278.4 5.5 %gather_fusion.5 = bf16[64,128,128]{2,1,0:T(8,128)(2,1)} fusion(bf16[4,64,128,128]{3,2,1,0:T(8,128)(2,1)} %all-gather.15.cloned.1.call-done, s32[64]{0:T(128)S(1)} %reshape.106), kind=kCustom, calls=%fused_computation.5.clone | custom fusion | bytes 4194816 | tf_op jit(solution)/shard_map/vmap(jit(_take))/gather | solution.py:8
  283.9 2.6 fusion.13
  286.5 0.3 copy-done.1
  286.8 0.1 copy-done.9
  286.9 0.8 fusion.32
  287.7 2.6 all_gather.37
  290.3 0.0 all-gather.17.cloned.1.call-update
  290.4 0.0 copy-start.3
  290.4 65.8 %all-gather.11.cloned.1.call-done = bf16[4,64,128,128]{3,2,1,0:T(8,128)(2,1)} async-done(((bf16[4,4,128,128]{3,2,1,0:T(8,128)(2,1)}), bf16[4,64,128,128]{3,2,1,0:T(8,128)(2,1)}) %all-gather.11.cloned.1.call-update) | async-done | bytes 8388624 | tf_op jit(solution)/shard_map/all_gather | solution.py:90
  356.2 4.3 gather_fusion.3
  360.6 2.6 fusion.31
  363.2 2.5 all_gather.34
  365.7 1.6 fusion.12
  367.3 66.7 %all-gather.17.cloned.1.call-done = bf16[4,64,128,128]{3,2,1,0:T(8,128)(2,1)} async-done(((bf16[4,4,128,128]{3,2,1,0:T(8,128)(2,1)}), bf16[4,64,128,128]{3,2,1,0:T(8,128)(2,1)}) %all-gather.17.cloned.1.call-update) | async-done | bytes 8388624 | tf_op jit(solution)/shard_map/all_gather | solution.py:91
  434.0 4.3 gather_fusion.6
  438.4 2.5 fusion.33
  440.9 2.5 all_gather.39
  443.4 0.8 copy.21
  444.2 0.8 copy.22
  (20 shorter events, 0.1 us)
Async XLA Ops:
  7.2 2.9 copy-start.6
  7.2 3.0 copy-start.5
  7.2 4.9 %copy-start.7 = (s32[4,4]{1,0:T(4,128)S(1)}, s32[4,4]{1,0:T(4,128)}, u32[]{:S(2)}) copy-start(s32[4,4]{1,0:T(4,128)} %param.23) | copy-start | bytes 196
  7.2 61.3 %all-gather.7.cloned.1.call-start = ((), (), s32[]{:S(2)}) async-start(), calls=%async_computation | async-start | bytes 4718592 | tf_op jit(solution)/shard_map/all_gather | solution.py:62
  7.9 137.4 %all-gather.9.cloned.1.call-start = ((), (), s32[]{:S(2)}) async-start(), calls=%async_computation.1 | async-start | bytes 8912896 | tf_op jit(solution)/shard_map/all_gather | solution.py:80
  8.7 193.0 %all-gather.13.cloned.1.call-start = ((), (), s32[]{:S(2)}) async-start(), calls=%async_computation.3 | async-start | bytes 4718592 | tf_op jit(solution)/shard_map/all_gather | solution.py:63
  9.4 269.0 %all-gather.15.cloned.1.call-start = ((), (), s32[]{:S(2)}) async-start(), calls=%async_computation.4 | async-start | bytes 8912896 | tf_op jit(solution)/shard_map/all_gather | solution.py:81
  10.0 346.2 %all-gather.11.cloned.1.call-start = ((), (), s32[]{:S(2)}) async-start(), calls=%async_computation.2 | async-start | bytes 8912896 | tf_op jit(solution)/shard_map/all_gather | solution.py:90
  72.9 76.8 %copy-start.8 = (bf16[4,4,128,128]{3,2,1,0:T(8,128)(2,1)S(1)}, bf16[4,4,128,128]{3,2,1,0:T(8,128)(2,1)}, u32[]{:S(2)}) copy-start(bf16[4,4,128,128]{3,2,1,0:T(8,128)(2,1)} %param.18) | copy-start | bytes 1572868
  154.8 279.3 %all-gather.17.cloned.1.call-start = ((), (), s32[]{:S(2)}) async-start(), calls=%async_computation.5 | async-start | bytes 8912896 | tf_op jit(solution)/shard_map/all_gather | solution.py:91
  283.9 2.6 copy-start
  283.9 2.9 copy-start.1
  283.9 2.9 copy-start.9
  290.4 70.2 %copy-start.3 = (bf16[4,4,128,128]{3,2,1,0:T(8,128)(2,1)S(1)}, bf16[4,4,128,128]{3,2,1,0:T(8,128)(2,1)}, u32[]{:S(2)}) copy-start(bf16[4,4,128,128]{3,2,1,0:T(8,128)(2,1)} %param.19) | copy-start | bytes 1572868
  360.6 5.1 %copy-start.2 = (bf16[8,8,128,128]{3,2,1,0:T(8,128)(2,1)S(1)}, bf16[8,8,128,128]{3,2,1,0:T(8,128)(2,1)}, u32[]{:S(2)}) copy-start(bf16[8,8,128,128]{3,2,1,0:T(8,128)(2,1)} %gather_fusion.4) | copy-start | bytes 6291460
  367.3 71.1 %copy-start.4 = (bf16[4,4,128,128]{3,2,1,0:T(8,128)(2,1)S(1)}, bf16[4,4,128,128]{3,2,1,0:T(8,128)(2,1)}, u32[]{:S(2)}) copy-start(bf16[4,4,128,128]{3,2,1,0:T(8,128)(2,1)} %param.21) | copy-start | bytes 1572868
Sparse Core Ops, SparseCore 0:
  9.8 58.6 all-gather.6
  70.9 74.3 all-gather.8
  147.1 54.5 all-gather.12
  204.0 74.3 all-gather.14
  280.7 75.4 all-gather.10
  358.5 75.4 all-gather.16
where the time goes:
time: 452 us
  waiting for transfers between devices  383 us (85%)
  local copies, waits for them, and re-layouts  30 us (7%)
  between operations  14.3 us (3%)
  matrix products  12.6 us (3%)
  blocking collectives  10.2 us (2%)
    all_gather x1, waiting for transfers between devices, on_device(): lax.all_gather(cheb_cur, 'row', axis=1, tiled=True)  72.5 us
    all_gather x1, waiting for transfers between devices, on_device(): lax.all_gather(tang_cur, 'row', axis=1, tiled=True)  72.3 us
    all_gather x1, waiting for transfers between devices, on_device(): lax.all_gather(tang_full, 'row', axis=1, tiled=True)  66.7 us
    all_gather x1, waiting for transfers between devices, on_device(): lax.all_gather(cheb_full, 'row', axis=1, tiled=True)  65.8 us
    all_gather x1, waiting for transfers between devices, on_device(): lax.all_gather(ham_rows, 'col', axis=1, tiled=True)  56 us
    all_gather x1, waiting for transfers between devices, on_device(): lax.all_gather(deriv_rows, 'col', axis=1, tiled=True)  46.9 us
    gather x5, local copies, waits for them, and re-layouts, pick_blocks(): return jnp.take(blocks, index, axis=0)  18.6 us
  transfers between devices with their start and end apart: 6, of which 6 were waited for; matrix products, arithmetic and copies ran while one was open for 8% of the time, Pallas kernels for 0%

commit v1 on v0

v1 whole, which is shorter than its diff:
```python
import functools

import jax
import jax.numpy as jnp
from jax import lax
from jax.experimental import pallas as pl
from jax.experimental.pallas import tpu as pltpu
from jax.sharding import PartitionSpec as P

ROWS, COLS, CORES = 16, 8, 2


def ring(shift):
    return [(i, (i + shift) % COLS) for i in range(COLS)]


def z_ring(blocks):
    half = blocks.shape[0] // 2
    up, down = [blocks], [blocks]
    for _ in range(3):
        up.append(lax.ppermute(up[-1], "col", ring(1)))
        down.append(lax.ppermute(down[-1], "col", ring(-1)))
    far_low = lax.ppermute(up[-1][:half], "col", ring(1))
    far_high = lax.ppermute(down[-1][half:], "col", ring(-1))
    pieces = [None] * COLS
    pieces[0] = [blocks]
    for step in range(1, 4):
        pieces[COLS - step] = [up[step]]
        pieces[step] = [down[step]]
    pieces[4] = [far_low, far_high]
    return pieces


def swap(array):
    return lax.ppermute(array, "depth", [(0, 1), (1, 0)])


def combine_kernel(pos, rowin, tpos, keep, *refs):
    ham = refs[:36]
    panel, cheb_old, tang_old, cheb_new, tang_new, buf, acc, sems = refs[36:]

    def parts(kind, owner, z):
        base = (kind * 2 + owner) * 9
        if z == 4:
            return ham[base + 7], ham[base + 8]
        return (ham[base + (z if z < 4 else z - 1)],)

    def ham_copy(ref, row, slot, kind):
        return pltpu.make_async_copy(ref.at[row], buf.at[slot, kind], sems.at[slot, kind])

    def panel_copy(place, out, slot, kind):
        column = lax.shift_right_logical(out, 1) & 1
        source = panel.at[lax.shift_right_logical(place, 2), kind, column, place & 3]
        return pltpu.make_async_copy(source, buf.at[slot, 2 + kind], sems.at[slot, 2 + kind])

    for owner in range(2):
        for z in range(COLS):

            def issue(i, carry, owner=owner, z=z):
                out = owner * 4 + i
                slot = out * COLS + z
                place = pos[slot]

                @pl.when(place >= 0)
                def _():
                    row = rowin[out]
                    for kind in range(2):
                        panel_copy(place, out, slot, kind).start()
                        refs_z = parts(kind, owner, z)
                        if len(refs_z) == 1:
                            ham_copy(refs_z[0], row, slot, kind).start()
                        else:

                            @pl.when(row < 8)
                            def _(kind=kind, refs_z=refs_z):
                                ham_copy(refs_z[0], row, slot, kind).start()

                            @pl.when(row >= 8)
                            def _(kind=kind, refs_z=refs_z):
                                ham_copy(refs_z[1], row - 8, slot, kind).start()

                return carry

            lax.fori_loop(0, 4, issue, 0)

    acc[...] = jnp.zeros_like(acc)

    def work(slot, carry):
        @pl.when(pos[slot] >= 0)
        def _():
            out = lax.shift_right_logical(slot, 3)
            for kind in range(2):
                ham_copy(ham[0], 0, slot, kind).wait()
                panel_copy(0, 0, slot, kind).wait()
            h, d, x, t = (buf[slot, i] for i in range(4))
            dot = functools.partial(jnp.dot, preferred_element_type=jnp.float32)
            acc[out, 0] += dot(h, x)
            acc[out, 1] += dot(d, x) + dot(h, t)

        return carry

    lax.fori_loop(0, 64, work, 0)

    def finish(out, carry):
        column = lax.shift_right_logical(out, 1) & 1
        t = tpos[out]
        scale = keep[out].astype(jnp.float32)
        old = cheb_old[column, t].astype(jnp.float32)
        cheb_new[column, t] = (scale * (2.0 * acc[out, 0] - old)).astype(jnp.bfloat16)
        old = tang_old[column, t].astype(jnp.float32)
        tang_new[column, t] = (scale * (2.0 * acc[out, 1] - old)).astype(jnp.bfloat16)
        return carry

    lax.fori_loop(0, 8, finish, 0)


def combine(tables, ham_pieces, panel, cheb_old, tang_old):
    any_space = pl.BlockSpec(memory_space=pl.ANY)
    vmem = pl.BlockSpec(memory_space=pltpu.VMEM)
    smem = pl.BlockSpec(memory_space=pltpu.SMEM)
    shape = jax.ShapeDtypeStruct(cheb_old.shape, jnp.bfloat16)
    return pl.pallas_call(
        combine_kernel,
        out_shape=(shape, shape),
        in_specs=[smem] * 4 + [any_space] * 37 + [vmem] * 2,
        out_specs=(vmem, vmem),
        scratch_shapes=[
            pltpu.VMEM((64, 4, 128, 128), jnp.bfloat16),
            pltpu.VMEM((8, 2, 128, 128), jnp.float32),
            pltpu.SemaphoreType.DMA((64, 4)),
        ],
        compiler_params=pltpu.CompilerParams(vmem_limit_bytes=24 * 1024 * 1024),
        cost_estimate=pl.CostEstimate(flops=100_000_000, bytes_accessed=4_000_000, transcendentals=0),
    )(*tables, *ham_pieces, panel, cheb_old, tang_old)


def needs(my_rows, ham_cols, other_cols, row_group, layer, col):
    rows = lax.dynamic_slice_in_dim(my_rows, row_group * 4, 4, 1)
    by_group = rows.reshape(2, 2, 2).transpose(1, 0, 2)
    by_owner = jnp.where(layer == 0, by_group, by_group[::-1])
    group = jnp.stack([layer, 1 - layer])
    row_in = by_owner - row_group * 32 - 16 * group[:, None, None]
    cols = jnp.stack([ham_cols, other_cols])
    onehot = row_in[..., None] == jnp.arange(16, dtype=jnp.int32)
    needed = jnp.sum(jnp.where(onehot[..., None], cols[:, None, None], 0), axis=3)
    order = (col + jnp.arange(8, dtype=jnp.int32)) % 8
    turn = order[:, None] == jnp.arange(8, dtype=jnp.int32)
    needed = jnp.sum(jnp.where(turn, needed[..., None, :], 0), axis=-1)
    equal = needed[..., None] == my_rows[None, :, None, None, :]
    place = jnp.max(jnp.where(equal, jnp.arange(64, dtype=jnp.int32), -1), axis=-1)
    return place, row_in, group


def on_device(
    ham_blocks,
    deriv_blocks,
    ham_cols,
    cheb_prev,
    cheb_cur,
    tang_prev,
    tang_cur,
    cheb_rows,
    keep_mask,
):
    layer = lax.axis_index("depth")
    row_group = lax.axis_index("row")
    col = lax.axis_index("col")

    def mine(array):
        return lax.dynamic_slice_in_dim(array, 2 * layer, 2, 0)

    my_rows, my_keep = mine(cheb_rows), mine(keep_mask)
    place, row_in, group = needs(my_rows, ham_cols, swap(ham_cols), row_group, layer, col)
    slots = jnp.broadcast_to(
        (2 * group[:, None, None] + jnp.arange(2, dtype=jnp.int32)[None, None, :]), (2, 2, 2)
    )
    keep_by_group = my_keep.reshape(2, 2, 2).transpose(1, 0, 2)
    keep = jnp.where(layer == 0, keep_by_group, keep_by_group[::-1])
    tables = (place.reshape(-1), row_in.reshape(-1), slots.reshape(-1), keep.reshape(-1))

    ham_pieces = []
    for blocks in (ham_blocks[:, 0], deriv_blocks[:, 0]):
        pieces = z_ring(blocks)
        flat = [pieces[z][0] for z in range(8) if z != 4] + pieces[4]
        ham_pieces += flat + [swap(piece) for piece in flat]

    def panel_of(cheb, tang):
        return lax.all_gather(jnp.stack([cheb, tang]), "row", axis=0)

    cheb, tang = mine(cheb_cur), mine(tang_cur)
    panel = panel_of(cheb, tang)
    cheb_mid, tang_mid = combine(tables, ham_pieces, panel, mine(cheb_prev), mine(tang_prev))
    panel = panel_of(cheb_mid, tang_mid)
    cheb_new, tang_new = combine(tables, ham_pieces, panel, cheb, tang)
    return (
        lax.all_gather(cheb_new, "depth", axis=0, tiled=True),
        lax.all_gather(tang_new, "depth", axis=0, tiled=True),
    )


def solution(mesh):
    placed = (
        P(("row", "depth"), "col", None, None),
        P(("row", "depth"), "col", None, None),
        P(("row", "depth"), None),
        P("col", "row", None, None),
        P("col", "row", None, None),
        P("col", "row", None, None),
        P("col", "row", None, None),
        P("col", None),
        P("col", "row"),
    )
    return jax.shard_map(
        on_device,
        mesh=mesh,
        in_specs=placed,
        out_specs=(P("col", "row", None, None), P("col", "row", None, None)),
        check_vma=False,
    )
```

time: 452 us -> 251 us (0.56)
  waiting for transfers between devices: 383 us -> 125 us
  starting transfers between devices: 0.23 us -> 34.9 us
  local copies, waits for them, and re-layouts: 30 us -> 53.1 us
  matrix products: 12.6 us -> 0 us
  Pallas kernels: 0 us -> 12.3 us
    all_gather x6 -> x2, waiting for transfers between devices: 380 us -> 78 us  [panel_of(): return lax.all_gather(jnp.stack([cheb, tang]), 'row', axis=0)]
    ppermute x0 -> x35, waiting for transfers between devices: none -> 47.1 us  [the longest x6 36.6 us: z_ring(): up.append(lax.ppermute(up[-1], 'col', ring(1)))]
    unnamed x23 -> x92, local copies, waits for them, and re-layouts: 2.05 us -> 47.2 us
    ppermute x0 -> x35, starting transfers between devices: none -> 34.8 us  [the longest x19 17.1 us: swap(): return lax.ppermute(array, 'depth', [(0, 1), (1, 0)])]
    gather x8 -> x0, local copies, waits for them, and re-layouts: 27.9 us -> none  [the longest x5 18.6 us: pick_blocks(): return jnp.take(blocks, index, axis=0)]
    dot_general x6 -> x0, matrix products: 12.6 us -> none  [the longest x2 5.04 us: select_terms(): jnp.einsum('jsqab,jsqbc->jsac', picked_ham, picked_cheb, preferred_elemen...]
    pallas_call x0 -> x2, Pallas kernels: none -> 12.3 us  [combine(): pl.pallas_call(combine_kernel, out_shape=(shape, shape), in_specs=[smem]...]
    all_gather x4 -> x2, blocking collectives: 10.2 us -> 7.23 us  [the longest x1 5.06 us: on_device(): lax.all_gather(cheb_new, 'depth', axis=0, tiled=True)]
  transfers between devices with their start and end apart: 6 -> 37, of which waited for: 6 -> 13; matrix products, arithmetic and copies ran while one was open for 8% -> 3% of each run, Pallas kernels for 0% -> 0%
where the time goes in v1:
time: 251 us; the launch traced here: 250 us
  waiting for transfers between devices  125 us (50%)
  local copies, waits for them, and re-layouts  53.1 us (21%)
  starting transfers between devices  34.9 us (14%)
  between operations  14.3 us (6%)
  Pallas kernels  12.3 us (5%)
  blocking collectives  7.23 us (3%)
  other arithmetic  3.53 us (1%)
    all_gather x2, waiting for transfers between devices, panel_of(): return lax.all_gather(jnp.stack([cheb, tang]), 'row', axis=0)  78 us
    unnamed x92, local copies, waits for them, and re-layouts  47.2 us
    ppermute x6, waiting for transfers between devices, z_ring(): up.append(lax.ppermute(up[-1], 'col', ring(1)))  36.6 us
    ppermute x19, starting transfers between devices, swap(): return lax.ppermute(array, 'depth', [(0, 1), (1, 0)])  17.1 us
    ppermute x6, starting transfers between devices, z_ring(): down.append(lax.ppermute(down[-1], 'col', ring(-1)))  13.5 us
    pallas_call x2, Pallas kernels, combine(): pl.pallas_call(combine_kernel, out_shape=(shape, shape), in_specs=[smem]...  12.3 us
    ppermute x6, waiting for transfers between devices, z_ring(): down.append(lax.ppermute(down[-1], 'col', ring(-1)))  6.35 us
    all_gather x1, blocking collectives, on_device(): lax.all_gather(cheb_new, 'depth', axis=0, tiled=True)  5.06 us
  transfers between devices with their start and end apart: 37, of which 13 were waited for; matrix products, arithmetic and copies ran while one was open for 3% of the time, Pallas kernels for 0%

profile of v1, /device:TPU:1, one launch (start us, length us, event | category | flops | bytes accessed | tf_op | source)
XLA Modules:
  0.0 250.5 jit_solution(8715750247694863974)
XLA Ops:
  7.2 1.1 constant_dynamic-slice_fusion.2
  9.3 3.3 %collective-permute-start.9 = (bf16[16,128,128]{2,1,0:T(8,128)(2,1)}, bf16[16,128,128]{2,1,0:T(8,128)(2,1)S(1)}, u32[]{:S(2)}, u32[]{:S(2)}) collective-permute-start(bf16[16,128,128]{2,1,0:T(8,128)(2,1)} %bitcast.20), channel_id=1, source_target_pairs={{0,1},{1,0},{2,3},{3,2},{4,5},{5,4},{6,7},{7,6},{8,9},{9,8},{10,11... | collective-permute-start | bytes 1572872 | tf_op jit(solution)/shard_map/ppermute | solution.py:35
  12.6 3.8 %collective-permute-start.1 = (bf16[16,128,128]{2,1,0:T(8,128)(2,1)}, bf16[16,128,128]{2,1,0:T(8,128)(2,1)S(1)}, u32[]{:S(2)}, u32[]{:S(2)}) collective-permute-start(bf16[16,128,128]{2,1,0:T(8,128)(2,1)} %bitcast.22), channel_id=1, source_target_pairs={{0,14},{2,0},{4,2},{6,4},{8,6},{10,8},{12,10},{14,12},{1,15},{3,1}... | collective-permute-start | bytes 1572872 | tf_op jit(solution)/shard_map/ppermute | solution.py:22
  18.7 2.7 %collective-permute-start.18 = (bf16[16,128,128]{2,1,0:T(8,128)(2,1)}, bf16[16,128,128]{2,1,0:T(8,128)(2,1)}, u32[]{:S(2)}, u32[]{:S(2)}) collective-permute-start(bf16[16,128,128]{2,1,0:T(8,128)(2,1)} %bitcast.27), channel_id=1, source_target_pairs={{0,14},{2,0},{4,2},{6,4},{8,6},{10,8},{12,10},{14,12},{1,15},{3,1}... | collective-permute-start | bytes 1572872 | tf_op jit(solution)/shard_map/ppermute | solution.py:22
  21.4 7.4 %collective-permute-done.4.refs_6_ = bf16[16,128,128]{2,1,0:T(8,128)(2,1)S(1)} collective-permute-done((bf16[16,128,128]{2,1,0:T(8,128)(2,1)}, bf16[16,128,128]{2,1,0:T(8,128)(2,1)S(1)}, u32[]{:S(2)}, u32[]{:S(2)}) %collective-permute-start.4) | collective-permute-done | bytes 524320 | tf_op jit(solution)/shard_map/ppermute | solution.py:21
  31.4 8.6 %collective-permute-done.21.refs_24_ = bf16[16,128,128]{2,1,0:T(8,128)(2,1)S(1)} collective-permute-done((bf16[16,128,128]{2,1,0:T(8,128)(2,1)}, bf16[16,128,128]{2,1,0:T(8,128)(2,1)S(1)}, u32[]{:S(2)}, u32[]{:S(2)}) %collective-permute-start.21) | collective-permute-done | bytes 524320 | tf_op jit(solution)/shard_map/ppermute | solution.py:21
  40.1 1.4 collective-permute-start.2
  42.3 1.5 collective-permute-start.32
  45.4 6.0 %collective-permute-done.5.refs_5_ = bf16[16,128,128]{2,1,0:T(8,128)(2,1)} collective-permute-done((bf16[16,128,128]{2,1,0:T(8,128)(2,1)S(1)}, bf16[16,128,128]{2,1,0:T(8,128)(2,1)}, u32[]{:S(2)}, u32[]{:S(2)}) %collective-permute-start.5) | collective-permute-done | bytes 524320 | tf_op jit(solution)/shard_map/ppermute | solution.py:21
  53.2 1.7 collective-permute-start.19
  56.7 2.6 %collective-permute-start.3 = (bf16[16,128,128]{2,1,0:T(8,128)(2,1)S(1)}, bf16[16,128,128]{2,1,0:T(8,128)(2,1)S(1)}, u32[]{:S(2)}, u32[]{:S(2)}) collective-permute-start(bf16[16,128,128]{2,1,0:T(8,128)(2,1)S(1)} %collective-permute-done.2.refs_2_), channel_id=1, source_target_pairs={{0,14},{2,0},{4,2},{6,4},{8,6},{10,8},{12,10},{14,12},{1,15},{3,1}... | collective-permute-start | bytes 1572872 | tf_op jit(solution)/shard_map/ppermute | solution.py:22
  59.3 3.3 %collective-permute-done.22.refs_23_ = bf16[16,128,128]{2,1,0:T(8,128)(2,1)} collective-permute-done((bf16[16,128,128]{2,1,0:T(8,128)(2,1)S(1)}, bf16[16,128,128]{2,1,0:T(8,128)(2,1)}, u32[]{:S(2)}, u32[]{:S(2)}) %collective-permute-start.22) | collective-permute-done | bytes 524320 | tf_op jit(solution)/shard_map/ppermute | solution.py:21
  64.5 2.5 collective-permute-done.19.refs_20_
  67.0 1.2 collective-permute-start.11
  68.2 5.7 %collective-permute-done.6.refs_4_ = bf16[16,128,128]{2,1,0:T(8,128)(2,1)S(1)} collective-permute-done((bf16[16,128,128]{2,1,0:T(8,128)(2,1)}, bf16[16,128,128]{2,1,0:T(8,128)(2,1)S(1)}, u32[]{:S(2)}, u32[]{:S(2)}) %collective-permute-start.6) | collective-permute-done | bytes 524320 | tf_op jit(solution)/shard_map/ppermute | solution.py:21
  73.9 1.3 collective-permute-start.20
  75.2 3.1 %collective-permute-done.3.refs_3_ = bf16[16,128,128]{2,1,0:T(8,128)(2,1)S(1)} collective-permute-done((bf16[16,128,128]{2,1,0:T(8,128)(2,1)S(1)}, bf16[16,128,128]{2,1,0:T(8,128)(2,1)S(1)}, u32[]{:S(2)}, u32[]{:S(2)}) %collective-permute-start.3) | collective-permute-done | bytes 524320 | tf_op jit(solution)/shard_map/ppermute | solution.py:22
  78.3 1.1 collective-permute-start.31
  79.6 5.6 %collective-permute-done.23.refs_22_ = bf16[16,128,128]{2,1,0:T(8,128)(2,1)S(1)} collective-permute-done((bf16[16,128,128]{2,1,0:T(8,128)(2,1)}, bf16[16,128,128]{2,1,0:T(8,128)(2,1)S(1)}, u32[]{:S(2)}, u32[]{:S(2)}) %collective-permute-start.23) | collective-permute-done | bytes 524320 | tf_op jit(solution)/shard_map/ppermute | solution.py:21
  85.1 1.3 collective-permute-start.8
  87.2 1.5 collective-permute-start.28
  91.1 2.9 %collective-permute-start.25 = (bf16[8,128,128]{2,1,0:T(8,128)(2,1)}, bf16[8,128,128]{2,1,0:T(8,128)(2,1)}, u32[]{:S(2)}, u32[]{:S(2)}) collective-permute-start(bf16[8,128,128]{2,1,0:T(8,128)(2,1)} %slice.19), channel_id=1, source_target_pairs={{0,14},{2,0},{4,2},{6,4},{8,6},{10,8},{12,10},{14,12},{1,15},{3,1}... | collective-permute-start | bytes 786440 | tf_op jit(solution)/shard_map/ppermute | solution.py:24
  94.0 1.4 collective-permute-start.16
  96.4 1.6 collective-permute-done.24.refs_25_
  98.0 1.8 collective-permute-start.33
  99.7 1.9 constant_dynamic-slice_fusion
  105.3 1.5 collective-permute-done.34.refs_35_
  106.9 3.4 %copy-done.1 = bf16[32,2,4,128,128]{4,3,2,1,0:T(8,128)(2,1)S(1)} copy-done((bf16[32,2,4,128,128]{4,3,2,1,0:T(8,128)(2,1)S(1)}, bf16[32,2,4,128,128]{4,3,2,1,0:T(8,128)(2,1)}, u32[]{:S(2)}) %copy-start.1) | copy-done | bytes 8388632
  110.2 1.0 copy-done.3
  111.3 1.0 copy-done.5
  112.3 1.0 copy-done.8
  114.4 1.0 copy-done.14
  115.4 1.0 copy-done.17
  118.6 1.0 copy-done.26
  119.6 1.0 copy-done.29
  121.7 1.0 copy-done.35
  122.7 1.0 copy-done.38
  123.8 1.0 copy-done.41
  126.7 6.1 %shard_map.104 = (bf16[2,4,128,128]{3,2,1,0:T(8,128)(2,1)S(1)}, bf16[2,4,128,128]{3,2,1,0:T(8,128)(2,1)S(1)}) custom-call(s32[64]{0:T(128)S(1)} %reshape.104.pos, s32[8]{0:T(128)S(1)} %reshape.105.rowin, s32[8]{0:T(128)S(1)} %reshape.106.tpos, s32[8]{0:T(128)S(1)} %reshape.108.keep, bf16[16,128,128]{2,1,0:T(8,128)(2,1)S(1)} %bitcast.23, ...), custom_call_target="tpu_custom_call" | custom-call | flops 100000000 | bytes 4000000 | tf_op jit(solution)/shard_map/pallas_call | solution.py:122
  133.8 78.0 %all-gather.7.cloned.1.call-done = bf16[32,2,4,128,128]{4,3,2,1,0:T(8,128)(2,1)} async-done(((bf16[2,2,4,128,128]{4,3,2,1,0:T(8,128)(2,1)}), bf16[32,2,4,128,128]{4,3,2,1,0:T(8,128)(2,1)}) %all-gather.7.cloned.1.call-update) | async-done | bytes 8388624 | tf_op jit(solution)/shard_map/all_gather | solution.py:188
  211.7 3.4 %copy-done.2 = bf16[32,2,4,128,128]{4,3,2,1,0:T(8,128)(2,1)S(1)} copy-done((bf16[32,2,4,128,128]{4,3,2,1,0:T(8,128)(2,1)S(1)}, bf16[32,2,4,128,128]{4,3,2,1,0:T(8,128)(2,1)}, u32[]{:S(2)}) %copy-start.2) | copy-done | bytes 8388632
  217.2 1.0 copy-done.12
  218.3 1.0 copy-done.15
  220.3 1.0 copy-done.21
  221.4 1.0 copy-done.24
  228.7 6.1 %shard_map.105 = (bf16[2,4,128,128]{3,2,1,0:T(8,128)(2,1)S(1)}, bf16[2,4,128,128]{3,2,1,0:T(8,128)(2,1)S(1)}) custom-call(s32[64]{0:T(128)S(1)} %reshape.104.pos, s32[8]{0:T(128)S(1)} %reshape.105.rowin, s32[8]{0:T(128)S(1)} %reshape.106.tpos, s32[8]{0:T(128)S(1)} %reshape.108.keep, bf16[16,128,128]{2,1,0:T(8,128)(2,1)S(1)} %bitcast.24, ...), custom_call_target="tpu_custom_call" | custom-call | flops 100000000 | bytes 4000000 | tf_op jit(solution)/shard_map/pallas_call | solution.py:122
  234.8 5.1 %all_gather.22 = bf16[4,4,128,128]{3,2,1,0:T(8,128)(2,1)S(1)} all-gather(bf16[2,4,128,128]{3,2,1,0:T(8,128)(2,1)S(1)} %get-tuple-element.8), channel_id=1, replica_groups=mesh['row'=16,'col'=8,'depth'=2] {'depth'}, dimensions={0}, use_global_device_ids=true | all-gather | bytes 786432 | tf_op jit(solution)/shard_map/all_gather | solution.py:196
  239.9 2.2 all_gather.23
  (157 shorter events, 39.7 us)
Async XLA Ops:
  7.2 57.2 %copy-start = (s32[4,4]{1,0:T(4,128)S(1)}, s32[4,4]{1,0:T(4,128)}, u32[]{:S(2)}) copy-start(s32[4,4]{1,0:T(4,128)} %param.17) | copy-start | bytes 196
  7.2 99.7 %all-gather.5.cloned.1.call-start = ((), (), s32[]{:S(2)}) async-start(), calls=%async_computation | async-start | bytes 8912896 | tf_op jit(solution)/shard_map/all_gather | solution.py:188
  9.2 202.5 %all-gather.7.cloned.1.call-start = ((), (), s32[]{:S(2)}) async-start(), calls=%async_computation.1 | async-start | bytes 8912896 | tf_op jit(solution)/shard_map/all_gather | solution.py:188
  9.3 8.7 %collective-permute-start.9 = (bf16[16,128,128]{2,1,0:T(8,128)(2,1)}, bf16[16,128,128]{2,1,0:T(8,128)(2,1)S(1)}, u32[]{:S(2)}, u32[]{:S(2)}) collective-permute-start(bf16[16,128,128]{2,1,0:T(8,128)(2,1)} %bitcast.20), channel_id=1, source_target_pairs={{0,1},{1,0},{2,3},{3,2},{4,5},{5,4},{6,7},{7,6},{8,9},{9,8},{10,11... | collective-permute-start | bytes 1572872 | tf_op jit(solution)/shard_map/ppermute | solution.py:35
  12.6 16.3 %collective-permute-start.4 = (bf16[16,128,128]{2,1,0:T(8,128)(2,1)}, bf16[16,128,128]{2,1,0:T(8,128)(2,1)S(1)}, u32[]{:S(2)}, u32[]{:S(2)}) collective-permute-start(bf16[16,128,128]{2,1,0:T(8,128)(2,1)} %bitcast.21), channel_id=1, source_target_pairs={{0,2},{2,4},{4,6},{6,8},{8,10},{10,12},{12,14},{14,0},{1,3},{3,5},... | collective-permute-start | bytes 1572872 | tf_op jit(solution)/shard_map/ppermute | solution.py:21
  12.6 17.2 %collective-permute-start.1 = (bf16[16,128,128]{2,1,0:T(8,128)(2,1)}, bf16[16,128,128]{2,1,0:T(8,128)(2,1)S(1)}, u32[]{:S(2)}, u32[]{:S(2)}) collective-permute-start(bf16[16,128,128]{2,1,0:T(8,128)(2,1)} %bitcast.22), channel_id=1, source_target_pairs={{0,14},{2,0},{4,2},{6,4},{8,6},{10,8},{12,10},{14,12},{1,15},{3,1}... | collective-permute-start | bytes 1572872 | tf_op jit(solution)/shard_map/ppermute | solution.py:22
  16.4 1.5 collective-permute-start
  16.9 13.7 %collective-permute-start.26 = (bf16[16,128,128]{2,1,0:T(8,128)(2,1)}, bf16[16,128,128]{2,1,0:T(8,128)(2,1)S(1)}, u32[]{:S(2)}, u32[]{:S(2)}) collective-permute-start(bf16[16,128,128]{2,1,0:T(8,128)(2,1)} %bitcast.25), channel_id=1, source_target_pairs={{0,1},{1,0},{2,3},{3,2},{4,5},{5,4},{6,7},{7,6},{8,9},{9,8},{10,11... | collective-permute-start | bytes 1572872 | tf_op jit(solution)/shard_map/ppermute | solution.py:35
  17.9 22.1 %collective-permute-start.21 = (bf16[16,128,128]{2,1,0:T(8,128)(2,1)}, bf16[16,128,128]{2,1,0:T(8,128)(2,1)S(1)}, u32[]{:S(2)}, u32[]{:S(2)}) collective-permute-start(bf16[16,128,128]{2,1,0:T(8,128)(2,1)} %bitcast.26), channel_id=1, source_target_pairs={{0,2},{2,4},{4,6},{6,8},{8,10},{10,12},{12,14},{14,0},{1,3},{3,5},... | collective-permute-start | bytes 1572872 | tf_op jit(solution)/shard_map/ppermute | solution.py:21
  18.7 23.5 %collective-permute-start.18 = (bf16[16,128,128]{2,1,0:T(8,128)(2,1)}, bf16[16,128,128]{2,1,0:T(8,128)(2,1)}, u32[]{:S(2)}, u32[]{:S(2)}) collective-permute-start(bf16[16,128,128]{2,1,0:T(8,128)(2,1)} %bitcast.27), channel_id=1, source_target_pairs={{0,14},{2,0},{4,2},{6,4},{8,6},{10,8},{12,10},{14,12},{1,15},{3,1}... | collective-permute-start | bytes 1572872 | tf_op jit(solution)/shard_map/ppermute | solution.py:22
  28.8 14.9 %collective-permute-start.15 = (bf16[16,128,128]{2,1,0:T(8,128)(2,1)S(1)}, bf16[16,128,128]{2,1,0:T(8,128)(2,1)S(1)}, u32[]{:S(2)}, u32[]{:S(2)}) collective-permute-start(bf16[16,128,128]{2,1,0:T(8,128)(2,1)S(1)} %collective-permute-done.4.refs_6_), channel_id=1, source_target_pairs={{0,1},{1,0},{2,3},{3,2},{4,5},{5,4},{6,7},{7,6},{8,9},{9,8},{10,11... | collective-permute-start | bytes 1572872 | tf_op jit(solution)/shard_map/ppermute | solution.py:35
  29.8 21.6 %collective-permute-start.5 = (bf16[16,128,128]{2,1,0:T(8,128)(2,1)S(1)}, bf16[16,128,128]{2,1,0:T(8,128)(2,1)}, u32[]{:S(2)}, u32[]{:S(2)}) collective-permute-start(bf16[16,128,128]{2,1,0:T(8,128)(2,1)S(1)} %collective-permute-done.4.refs_6_), channel_id=1, source_target_pairs={{0,2},{2,4},{4,6},{6,8},{8,10},{10,12},{12,14},{14,0},{1,3},{3,5},... | collective-permute-start | bytes 1572872 | tf_op jit(solution)/shard_map/ppermute | solution.py:21
  31.4 20.9 %collective-permute-start.10 = (bf16[16,128,128]{2,1,0:T(8,128)(2,1)S(1)}, bf16[16,128,128]{2,1,0:T(8,128)(2,1)S(1)}, u32[]{:S(2)}, u32[]{:S(2)}) collective-permute-start(bf16[16,128,128]{2,1,0:T(8,128)(2,1)S(1)} %collective-permute-done.1.refs_1_), channel_id=1, source_target_pairs={{0,1},{1,0},{2,3},{3,2},{4,5},{5,4},{6,7},{7,6},{8,9},{9,8},{10,11... | collective-permute-start | bytes 1572872 | tf_op jit(solution)/shard_map/ppermute | solution.py:35
  40.1 14.8 %collective-permute-start.2 = (bf16[16,128,128]{2,1,0:T(8,128)(2,1)S(1)}, bf16[16,128,128]{2,1,0:T(8,128)(2,1)S(1)}, u32[]{:S(2)}, u32[]{:S(2)}) collective-permute-start(bf16[16,128,128]{2,1,0:T(8,128)(2,1)S(1)} %collective-permute-done.1.refs_1_), channel_id=1, source_target_pairs={{0,14},{2,0},{4,2},{6,4},{8,6},{10,8},{12,10},{14,12},{1,15},{3,1}... | collective-permute-start | bytes 1572872 | tf_op jit(solution)/shard_map/ppermute | solution.py:22
  42.3 13.6 %collective-permute-start.32 = (bf16[16,128,128]{2,1,0:T(8,128)(2,1)S(1)}, bf16[16,128,128]{2,1,0:T(8,128)(2,1)S(1)}, u32[]{:S(2)}, u32[]{:S(2)}) collective-permute-start(bf16[16,128,128]{2,1,0:T(8,128)(2,1)S(1)} %collective-permute-done.21.refs_24_), channel_id=1, source_target_pairs={{0,1},{1,0},{2,3},{3,2},{4,5},{5,4},{6,7},{7,6},{8,9},{9,8},{10,11... | collective-permute-start | bytes 1572872 | tf_op jit(solution)/shard_map/ppermute | solution.py:35
  44.6 18.0 %collective-permute-start.22 = (bf16[16,128,128]{2,1,0:T(8,128)(2,1)S(1)}, bf16[16,128,128]{2,1,0:T(8,128)(2,1)}, u32[]{:S(2)}, u32[]{:S(2)}) collective-permute-start(bf16[16,128,128]{2,1,0:T(8,128)(2,1)S(1)} %collective-permute-done.21.refs_24_), channel_id=1, source_target_pairs={{0,2},{2,4},{4,6},{6,8},{8,10},{10,12},{12,14},{14,0},{1,3},{3,5},... | collective-permute-start | bytes 1572872 | tf_op jit(solution)/shard_map/ppermute | solution.py:21
  51.4 12.2 %collective-permute-start.27 = (bf16[16,128,128]{2,1,0:T(8,128)(2,1)}, bf16[16,128,128]{2,1,0:T(8,128)(2,1)S(1)}, u32[]{:S(2)}, u32[]{:S(2)}) collective-permute-start(bf16[16,128,128]{2,1,0:T(8,128)(2,1)} %collective-permute-done.18.refs_19_), channel_id=1, source_target_pairs={{0,1},{1,0},{2,3},{3,2},{4,5},{5,4},{6,7},{7,6},{8,9},{9,8},{10,11... | collective-permute-start | bytes 1572872 | tf_op jit(solution)/shard_map/ppermute | solution.py:35
  53.2 13.9 %collective-permute-start.19 = (bf16[16,128,128]{2,1,0:T(8,128)(2,1)}, bf16[16,128,128]{2,1,0:T(8,128)(2,1)}, u32[]{:S(2)}, u32[]{:S(2)}) collective-permute-start(bf16[16,128,128]{2,1,0:T(8,128)(2,1)} %collective-permute-done.18.refs_19_), channel_id=1, source_target_pairs={{0,14},{2,0},{4,2},{6,4},{8,6},{10,8},{12,10},{14,12},{1,15},{3,1}... | collective-permute-start | bytes 1572872 | tf_op jit(solution)/shard_map/ppermute | solution.py:22
  54.8 52.0 %copy-start.28 = (bf16[16,128,128]{2,1,0:T(8,128)(2,1)}, bf16[16,128,128]{2,1,0:T(8,128)(2,1)S(1)}, u32[]{:S(2)}) copy-start(bf16[16,128,128]{2,1,0:T(8,128)(2,1)S(1)} %collective-permute-done.2.refs_2_) | copy-start | bytes 1572868
  54.8 19.0 %collective-permute-start.6 = (bf16[16,128,128]{2,1,0:T(8,128)(2,1)}, bf16[16,128,128]{2,1,0:T(8,128)(2,1)S(1)}, u32[]{:S(2)}, u32[]{:S(2)}) collective-permute-start(bf16[16,128,128]{2,1,0:T(8,128)(2,1)} %collective-permute-done.5.refs_5_), channel_id=1, source_target_pairs={{0,2},{2,4},{4,6},{6,8},{8,10},{10,12},{12,14},{14,0},{1,3},{3,5},... | collective-permute-start | bytes 1572872 | tf_op jit(solution)/shard_map/ppermute | solution.py:21
  56.7 21.6 %collective-permute-start.3 = (bf16[16,128,128]{2,1,0:T(8,128)(2,1)S(1)}, bf16[16,128,128]{2,1,0:T(8,128)(2,1)S(1)}, u32[]{:S(2)}, u32[]{:S(2)}) collective-permute-start(bf16[16,128,128]{2,1,0:T(8,128)(2,1)S(1)} %collective-permute-done.2.refs_2_), channel_id=1, source_target_pairs={{0,14},{2,0},{4,2},{6,4},{8,6},{10,8},{12,10},{14,12},{1,15},{3,1}... | collective-permute-start | bytes 1572872 | tf_op jit(solution)/shard_map/ppermute | solution.py:22
  62.6 16.8 %collective-permute-start.14 = (bf16[16,128,128]{2,1,0:T(8,128)(2,1)}, bf16[16,128,128]{2,1,0:T(8,128)(2,1)}, u32[]{:S(2)}, u32[]{:S(2)}) collective-permute-start(bf16[16,128,128]{2,1,0:T(8,128)(2,1)} %collective-permute-done.5.refs_5_), channel_id=1, source_target_pairs={{0,1},{1,0},{2,3},{3,2},{4,5},{5,4},{6,7},{7,6},{8,9},{9,8},{10,11... | collective-permute-start | bytes 1572872 | tf_op jit(solution)/shard_map/ppermute | solution.py:35
  64.4 20.7 %collective-permute-start.23 = (bf16[16,128,128]{2,1,0:T(8,128)(2,1)}, bf16[16,128,128]{2,1,0:T(8,128)(2,1)S(1)}, u32[]{:S(2)}, u32[]{:S(2)}) collective-permute-start(bf16[16,128,128]{2,1,0:T(8,128)(2,1)} %collective-permute-done.22.refs_23_), channel_id=1, source_target_pairs={{0,2},{2,4},{4,6},{6,8},{8,10},{10,12},{12,14},{14,0},{1,3},{3,5},... | collective-permute-start | bytes 1572872 | tf_op jit(solution)/shard_map/ppermute | solution.py:21
  67.0 19.4 %collective-permute-start.11 = (bf16[16,128,128]{2,1,0:T(8,128)(2,1)S(1)}, bf16[16,128,128]{2,1,0:T(8,128)(2,1)S(1)}, u32[]{:S(2)}, u32[]{:S(2)}) collective-permute-start(bf16[16,128,128]{2,1,0:T(8,128)(2,1)S(1)} %collective-permute-done.2.refs_2_), channel_id=1, source_target_pairs={{0,1},{1,0},{2,3},{3,2},{4,5},{5,4},{6,7},{7,6},{8,9},{9,8},{10,11... | collective-permute-start | bytes 1572872 | tf_op jit(solution)/shard_map/ppermute | solution.py:35
  73.9 15.6 %collective-permute-start.20 = (bf16[16,128,128]{2,1,0:T(8,128)(2,1)}, bf16[16,128,128]{2,1,0:T(8,128)(2,1)S(1)}, u32[]{:S(2)}, u32[]{:S(2)}) collective-permute-start(bf16[16,128,128]{2,1,0:T(8,128)(2,1)} %collective-permute-done.19.refs_20_), channel_id=1, source_target_pairs={{0,14},{2,0},{4,2},{6,4},{8,6},{10,8},{12,10},{14,12},{1,15},{3,1}... | collective-permute-start | bytes 1572872 | tf_op jit(solution)/shard_map/ppermute | solution.py:22
  78.3 12.1 %collective-permute-start.31 = (bf16[16,128,128]{2,1,0:T(8,128)(2,1)}, bf16[16,128,128]{2,1,0:T(8,128)(2,1)S(1)}, u32[]{:S(2)}, u32[]{:S(2)}) collective-permute-start(bf16[16,128,128]{2,1,0:T(8,128)(2,1)} %collective-permute-done.22.refs_23_), channel_id=1, source_target_pairs={{0,1},{1,0},{2,3},{3,2},{4,5},{5,4},{6,7},{7,6},{8,9},{9,8},{10,11... | collective-permute-start | bytes 1572872 | tf_op jit(solution)/shard_map/ppermute | solution.py:35
  79.5 14.6 %collective-permute-start.7 = (bf16[8,128,128]{2,1,0:T(8,128)(2,1)S(1)}, bf16[8,128,128]{2,1,0:T(8,128)(2,1)S(1)}, u32[]{:S(2)}, u32[]{:S(2)}) collective-permute-start(bf16[8,128,128]{2,1,0:T(8,128)(2,1)S(1)} %slice.16), channel_id=1, source_target_pairs={{0,2},{2,4},{4,6},{6,8},{8,10},{10,12},{12,14},{14,0},{1,3},{3,5},... | collective-permute-start | bytes 786440 | tf_op jit(solution)/shard_map/ppermute | solution.py:23
  85.1 10.3 %collective-permute-start.8 = (bf16[8,128,128]{2,1,0:T(8,128)(2,1)S(1)}, bf16[8,128,128]{2,1,0:T(8,128)(2,1)}, u32[]{:S(2)}, u32[]{:S(2)}) collective-permute-start(bf16[8,128,128]{2,1,0:T(8,128)(2,1)S(1)} %slice.17), channel_id=1, source_target_pairs={{0,14},{2,0},{4,2},{6,4},{8,6},{10,8},{12,10},{14,12},{1,15},{3,1}... | collective-permute-start | bytes 786440 | tf_op jit(solution)/shard_map/ppermute | solution.py:24
  87.2 14.6 %collective-permute-start.28 = (bf16[16,128,128]{2,1,0:T(8,128)(2,1)}, bf16[16,128,128]{2,1,0:T(8,128)(2,1)}, u32[]{:S(2)}, u32[]{:S(2)}) collective-permute-start(bf16[16,128,128]{2,1,0:T(8,128)(2,1)} %collective-permute-done.19.refs_20_), channel_id=1, source_target_pairs={{0,1},{1,0},{2,3},{3,2},{4,5},{5,4},{6,7},{7,6},{8,9},{9,8},{10,11... | collective-permute-start | bytes 1572872 | tf_op jit(solution)/shard_map/ppermute | solution.py:35
  89.5 8.5 %collective-permute-start.24 = (bf16[8,128,128]{2,1,0:T(8,128)(2,1)S(1)}, bf16[8,128,128]{2,1,0:T(8,128)(2,1)}, u32[]{:S(2)}, u32[]{:S(2)}) collective-permute-start(bf16[8,128,128]{2,1,0:T(8,128)(2,1)S(1)} %slice.18), channel_id=1, source_target_pairs={{0,2},{2,4},{4,6},{6,8},{8,10},{10,12},{12,14},{14,0},{1,3},{3,5},... | collective-permute-start | bytes 786440 | tf_op jit(solution)/shard_map/ppermute | solution.py:23
  91.1 10.8 %collective-permute-start.25 = (bf16[8,128,128]{2,1,0:T(8,128)(2,1)}, bf16[8,128,128]{2,1,0:T(8,128)(2,1)}, u32[]{:S(2)}, u32[]{:S(2)}) collective-permute-start(bf16[8,128,128]{2,1,0:T(8,128)(2,1)} %slice.19), channel_id=1, source_target_pairs={{0,14},{2,0},{4,2},{6,4},{8,6},{10,8},{12,10},{14,12},{1,15},{3,1}... | collective-permute-start | bytes 786440 | tf_op jit(solution)/shard_map/ppermute | solution.py:24
  94.0 8.4 %collective-permute-start.16 = (bf16[8,128,128]{2,1,0:T(8,128)(2,1)S(1)}, bf16[8,128,128]{2,1,0:T(8,128)(2,1)}, u32[]{:S(2)}, u32[]{:S(2)}) collective-permute-start(bf16[8,128,128]{2,1,0:T(8,128)(2,1)S(1)} %collective-permute-done.7.refs_7_), channel_id=1, source_target_pairs={{0,1},{1,0},{2,3},{3,2},{4,5},{5,4},{6,7},{7,6},{8,9},{9,8},{10,11... | collective-permute-start | bytes 786440 | tf_op jit(solution)/shard_map/ppermute | solution.py:35
  95.4 7.1 %collective-permute-start.17 = (bf16[8,128,128]{2,1,0:T(8,128)(2,1)}, bf16[8,128,128]{2,1,0:T(8,128)(2,1)}, u32[]{:S(2)}, u32[]{:S(2)}) collective-permute-start(bf16[8,128,128]{2,1,0:T(8,128)(2,1)} %collective-permute-done.8.refs_8_), channel_id=1, source_target_pairs={{0,1},{1,0},{2,3},{3,2},{4,5},{5,4},{6,7},{7,6},{8,9},{9,8},{10,11... | collective-permute-start | bytes 786440 | tf_op jit(solution)/shard_map/ppermute | solution.py:35
  98.0 6.3 %collective-permute-start.33 = (bf16[8,128,128]{2,1,0:T(8,128)(2,1)}, bf16[8,128,128]{2,1,0:T(8,128)(2,1)}, u32[]{:S(2)}, u32[]{:S(2)}) collective-permute-start(bf16[8,128,128]{2,1,0:T(8,128)(2,1)} %collective-permute-done.24.refs_25_), channel_id=1, source_target_pairs={{0,1},{1,0},{2,3},{3,2},{4,5},{5,4},{6,7},{7,6},{8,9},{9,8},{10,11... | collective-permute-start | bytes 786440 | tf_op jit(solution)/shard_map/ppermute | solution.py:35
  101.9 4.9 %collective-permute-start.13 = (bf16[16,128,128]{2,1,0:T(8,128)(2,1)S(1)}, bf16[16,128,128]{2,1,0:T(8,128)(2,1)}, u32[]{:S(2)}, u32[]{:S(2)}) collective-permute-start(bf16[16,128,128]{2,1,0:T(8,128)(2,1)S(1)} %collective-permute-done.6.refs_4_), channel_id=1, source_target_pairs={{0,1},{1,0},{2,3},{3,2},{4,5},{5,4},{6,7},{7,6},{8,9},{9,8},{10,11... | collective-permute-start | bytes 1572872 | tf_op jit(solution)/shard_map/ppermute | solution.py:35
  101.9 4.9 %collective-permute-start.12 = (bf16[16,128,128]{2,1,0:T(8,128)(2,1)S(1)}, bf16[16,128,128]{2,1,0:T(8,128)(2,1)}, u32[]{:S(2)}, u32[]{:S(2)}) collective-permute-start(bf16[16,128,128]{2,1,0:T(8,128)(2,1)S(1)} %collective-permute-done.3.refs_3_), channel_id=1, source_target_pairs={{0,1},{1,0},{2,3},{3,2},{4,5},{5,4},{6,7},{7,6},{8,9},{9,8},{10,11... | collective-permute-start | bytes 1572872 | tf_op jit(solution)/shard_map/ppermute | solution.py:35
  102.4 4.4 %collective-permute-start.30 = (bf16[16,128,128]{2,1,0:T(8,128)(2,1)S(1)}, bf16[16,128,128]{2,1,0:T(8,128)(2,1)}, u32[]{:S(2)}, u32[]{:S(2)}) collective-permute-start(bf16[16,128,128]{2,1,0:T(8,128)(2,1)S(1)} %collective-permute-done.23.refs_22_), channel_id=1, source_target_pairs={{0,1},{1,0},{2,3},{3,2},{4,5},{5,4},{6,7},{7,6},{8,9},{9,8},{10,11... | collective-permute-start | bytes 1572872 | tf_op jit(solution)/shard_map/ppermute | solution.py:35
  102.5 4.3 %collective-permute-start.29 = (bf16[16,128,128]{2,1,0:T(8,128)(2,1)S(1)}, bf16[16,128,128]{2,1,0:T(8,128)(2,1)}, u32[]{:S(2)}, u32[]{:S(2)}) collective-permute-start(bf16[16,128,128]{2,1,0:T(8,128)(2,1)S(1)} %collective-permute-done.20.refs_21_), channel_id=1, source_target_pairs={{0,1},{1,0},{2,3},{3,2},{4,5},{5,4},{6,7},{7,6},{8,9},{9,8},{10,11... | collective-permute-start | bytes 1572872 | tf_op jit(solution)/shard_map/ppermute | solution.py:35
  104.3 2.5 collective-permute-start.34
  106.9 3.4 %copy-start.1 = (bf16[32,2,4,128,128]{4,3,2,1,0:T(8,128)(2,1)S(1)}, bf16[32,2,4,128,128]{4,3,2,1,0:T(8,128)(2,1)}, u32[]{:S(2)}) copy-start(bf16[32,2,4,128,128]{4,3,2,1,0:T(8,128)(2,1)} %all-gather.5.cloned.1.call-done) | copy-start | bytes 25165828
  110.2 1.0 copy-start.3
  111.3 1.0 copy-start.5
  112.3 1.0 copy-start.8
  113.4 1.0 copy-start.11
  114.4 1.0 copy-start.14
  115.4 1.0 copy-start.17
  126.7 85.0 %copy-start.4 = (bf16[16,1,128,128]{3,2,1,0:T(8,128)(2,1)S(1)}, bf16[16,1,128,128]{3,2,1,0:T(8,128)(2,1)}, u32[]{:S(2)}) copy-start(bf16[16,1,128,128]{3,2,1,0:T(8,128)(2,1)} %param.9) | copy-start | bytes 1572868
  211.7 3.4 %copy-start.2 = (bf16[32,2,4,128,128]{4,3,2,1,0:T(8,128)(2,1)S(1)}, bf16[32,2,4,128,128]{4,3,2,1,0:T(8,128)(2,1)}, u32[]{:S(2)}) copy-start(bf16[32,2,4,128,128]{4,3,2,1,0:T(8,128)(2,1)} %all-gather.7.cloned.1.call-done) | copy-start | bytes 25165828
  (34 other events, 32.7 us)
Sparse Core Ops, SparseCore 0:
  10.4 79.5 all-gather.4
  133.9 77.8 all-gather.6
